TPU v7x, 32 devices: a whole 2x2x4 slice. The times are simulated.
32 devices in a mesh: groups: 2 (over y), replica: 2 (over core), tensor: 8 (over z, x).
Axes of the slice: x: 2, y: 2, z: 4, core: 2. Of those that a mesh axis runs over, the one named last changes fastest.
Arguments:
- tokens: bfloat16 [2560, 8192], P(('groups', 'replica', 'tensor')), parts along dimension 0, may hold values from -6 to 6, as said below
- norm_scale_weight: float32 [8192], replicated, may hold values from 0.25 to 1.75
- query_weight: bfloat16 [128, 4096, 128], P('tensor'), may hold values from -0.06629126 to 0.06629126, as said below
- key_value_weight: bfloat16 [1024, 2, 8192], P('tensor'), may hold values from -0.06629126 to 0.06629126, as said below
- adapter_down_weight: bfloat16 [96, 8192, 128], P('replica', 'tensor'), may hold values from -0.0625 to 0.0625
- adapter_up_query: bfloat16 [96, 128, 32, 128], P('replica', 'tensor'), may hold values from -0.75 to 0.75
- adapter_up_value: bfloat16 [96, 65536], P('replica', 'tensor'), may hold values from -0.75 to 0.75
- request_adapter_index: int32 [4, 8], P('groups'), parts along dimension 0, may hold values from 0 to 95
- adapter_slot: int32 [96], replicated, may hold values from 0 to 95, each once
- request_row_lengths: int32 [4, 8], P('groups'), parts along dimension 0, may hold values from 1 to 160, 640 in all within a row
Outputs:
- context: bfloat16 [4, 128, 320, 128], P(('groups', 'replica'), 'tensor'), parts along dimension 0
There are 2 independent parts, one for each index of `groups`. A program takes and returns all parts, laid end to end along the dimension named above; an argument that names none is the same for every part. Nothing has to cross between parts.
Inputs may be any that keep to these rules, and one draw needn't show every extreme that they name: `request_adapter_index`: the adapter that each request uses; adapters may repeat. A permutation: adapter a is stored in slot adapter_slot[a], and slots r * 48 to (r + 1) * 48 - 1 are held by replica r. `request_row_lengths`: each row sums to 640; the requests of a replica cover its rows in order. `tokens`: drawn afresh for each group. `query_weight`: shared by all groups. `key_value_weight`: shared by all groups.
All inputs are finite; a program needn't handle non-finite values.
Results may differ from a plain program's by a relative error of at most 0.0092.
Values may be sent and summed in bfloat16 or wider, within the bound.
A program may use at most 192 MiB of HBM per device.

v0:
```python
import math

import jax
import jax.numpy as jnp
from jax import lax
from jax.sharding import PartitionSpec as P

QUERY_HEADS = 64
KEYVALUE_HEADS = 8
HEAD_WIDTH = 128


def partner_2(block, axis, apart):
    count = lax.axis_size(axis)
    route = []
    for low in range(count):
        high = low | 1 << apart
        if high != low and high < count:
            route += [(low, high), (high, low)]
    return lax.ppermute(block, axis, route)


def on_device(
    tokens,
    norm_scale_weight,
    query_weight,
    key_value_weight,
    adapter_down_weight,
    adapter_up_query,
    adapter_up_value,
    request_adapter_index,
    adapter_slot,
    request_row_lengths,
):
    shards = lax.axis_size("tensor")
    position = lax.axis_index("tensor")
    replica_now = lax.axis_index("replica")
    local_columns = adapter_down_weight.shape[1]
    complete_rank = adapter_down_weight.shape[2] // 2
    head_rows = query_weight.shape[0]
    half_width = query_weight.shape[1]
    head_length = query_weight.shape[2]
    half_rank_count = adapter_up_query.shape[2]
    value_cols = key_value_weight.shape[0]
    top_bit = shards.bit_length() - 2
    side = position // (shards // 2)
    first_head = position * head_rows - side * QUERY_HEADS
    widened = tokens.astype(jnp.float32)
    normed = (
        widened
        * lax.rsqrt(jnp.mean(widened * widened, axis=1, keepdims=True) + 1e-05)
        * norm_scale_weight
    ).astype(jnp.bfloat16)
    gathered_rows = lax.all_gather(normed, "tensor", axis=0, tiled=True)
    length_gathered = gathered_rows.shape[0]
    lengths_mine = lax.dynamic_index_in_dim(request_row_lengths, replica_now, 0, keepdims=False)
    seg_ends = jnp.cumsum(lengths_mine)
    seg_starts = seg_ends - lengths_mine
    row_index = jnp.arange(length_gathered, dtype=jnp.int32)
    member_mask = (row_index[:, None] >= seg_starts[None, :]) & (
        row_index[:, None] < seg_ends[None, :]
    )
    member_bf = member_mask.astype(jnp.bfloat16)
    segment_ids = jnp.sum((row_index[:, None] >= seg_ends[None, :]).astype(jnp.int32), axis=1)
    wanted = lax.dynamic_index_in_dim(request_adapter_index, replica_now, 0, keepdims=False)
    storage_slots = jnp.take(adapter_slot, wanted)
    gathered = (
        lax.all_gather(adapter_down_weight, "replica", axis=0, tiled=True),
        lax.all_gather(adapter_up_query, "replica", axis=0, tiled=True),
        lax.all_gather(adapter_up_value, "replica", axis=0, tiled=True),
    )
    fetched = tuple((jnp.take(store_part, storage_slots, axis=0) for store_part in gathered))
    down_sel, upq_sel, upv_sel = fetched
    requests = down_sel.shape[0]
    my_columns = lax.dynamic_slice_in_dim(gathered_rows, position * local_columns, local_columns, 1)
    down_mat = jnp.transpose(down_sel, (1, 0, 2)).reshape(
        local_columns, requests * 2 * complete_rank
    )
    per_request = jnp.dot(my_columns, down_mat, preferred_element_type=jnp.float32).reshape(
        length_gathered, requests, 2 * complete_rank
    )
    partial_down = jnp.sum(
        jnp.where(member_mask[:, :, None], per_request, jnp.float32(0.0)), axis=1
    )
    down_bf = lax.psum(partial_down, "tensor").astype(jnp.bfloat16)
    down_query = lax.dynamic_slice_in_dim(down_bf, side * half_rank_count, half_rank_count, 1)
    down_value = down_bf[:, complete_rank:]
    expand_query = (member_bf[:, :, None] * down_query[:, None, :]).reshape(
        length_gathered, requests * half_rank_count
    )
    upq_mat = jnp.transpose(upq_sel, (1, 0, 2, 3)).reshape(
        head_rows, requests * half_rank_count, head_length
    )
    my_features = lax.dynamic_slice_in_dim(gathered_rows, side * half_width, half_width, 1)
    partial_query = jnp.einsum(
        "tf,mfd->mtd", my_features, query_weight, preferred_element_type=jnp.float32
    )
    partial_query = partial_query + jnp.einsum(
        "tj,mjd->mtd", expand_query, upq_mat, preferred_element_type=jnp.float32
    )
    partner = partner_2(partial_query, "tensor", top_bit)
    query_all = (partial_query + partner).astype(jnp.bfloat16)
    kv_local = jnp.einsum(
        "ckf,tf->ckt", key_value_weight, gathered_rows, preferred_element_type=jnp.float32
    )
    expand_value = (member_bf[:, :, None] * down_value[:, None, :]).reshape(
        length_gathered, requests * complete_rank
    )
    upv_mat = jnp.transpose(
        upv_sel.reshape(requests, value_cols, complete_rank), (1, 0, 2)
    ).reshape(value_cols, requests * complete_rank)
    value_term = jnp.einsum("cj,tj->ct", upv_mat, expand_value, preferred_element_type=jnp.float32)
    key_value = jnp.stack([kv_local[:, 0], kv_local[:, 1] + value_term], axis=1).astype(
        jnp.bfloat16
    )
    key_value_gathered = lax.all_gather(key_value, "tensor", axis=0, tiled=True)
    key_value_heads = key_value_gathered.reshape(KEYVALUE_HEADS, head_length, 2, length_gathered)
    group_width = QUERY_HEADS // KEYVALUE_HEADS
    head_ids = (first_head + jnp.arange(head_rows, dtype=jnp.int32)) // group_width
    chosen_heads = jnp.take(key_value_heads, head_ids, axis=0)
    key_head_count = chosen_heads[:, :, 0]
    value_head_count = chosen_heads[:, :, 1]
    rows_here = length_gathered // 2
    query_seq = lax.dynamic_slice_in_dim(query_all, side * rows_here, rows_here, 1)
    query_index = side * rows_here + jnp.arange(rows_here, dtype=jnp.int32)
    query_segment = jnp.take(segment_ids, query_index)
    allowed = (row_index[None, :] <= query_index[:, None]) & (
        segment_ids[None, :] == query_segment[:, None]
    )
    scores = jnp.einsum(
        "mqd,mdk->mqk", query_seq, key_head_count, preferred_element_type=jnp.float32
    ) / math.sqrt(HEAD_WIDTH)
    scores = jnp.where(allowed[None], scores, jnp.float32(-1e30))
    row_max = jnp.max(scores, axis=-1, keepdims=True)
    weights = jnp.exp(scores - row_max)
    weights = (weights / jnp.sum(weights, axis=-1, keepdims=True)).astype(jnp.bfloat16)
    context = jnp.einsum(
        "mqk,mdk->mqd", weights, value_head_count, preferred_element_type=jnp.float32
    )
    return context[None].astype(jnp.bfloat16)


def solution(mesh):
    in_specs = (
        P(("groups", "replica", "tensor"), None),
        P(),
        P("tensor", None, None),
        P("tensor", None, None),
        P("replica", "tensor", None),
        P("replica", "tensor", None, None),
        P("replica", "tensor"),
        P("groups", None),
        P(),
        P("groups", None),
    )
    out_specs = P(("groups", "replica"), "tensor", None, None)
    return jax.shard_map(
        on_device, mesh=mesh, in_specs=in_specs, out_specs=out_specs, check_vma=False
    )
```

profile of v0, /device:TPU:12, one launch (start us, length us, event | category | flops | bytes accessed | tf_op | source)
XLA Modules:
  0.0 584.7 jit_solution(4248723410867543657)
XLA Ops:
  6.5 0.7 all-gather.12.cloned.1.call-update
  7.3 0.0 all-gather.8.cloned.1.call-start
  7.3 0.7 all-gather.8.cloned.1.call-update
  8.0 0.0 all-gather.6.cloned.1.call-start
  8.1 0.3 fusion.12
  8.4 1.4 fusion.14
  9.9 0.0 all-gather.6.cloned.1.call-update
  9.9 0.0 all-gather.10.cloned.1.call-start
  10.0 0.5 all-gather.10.cloned.1.call-update
  10.5 0.0 all-gather.14.cloned.1.call-start
  10.6 0.2 reduce-window.4
  10.8 0.6 gather_fusion.1
  11.5 0.1 fusion.86
  11.6 8.5 %all-gather.12.cloned.1.call-done = bf16[96,8192]{1,0:T(8,128)(2,1)} async-done(((bf16[48,8192]{1,0:T(8,128)(2,1)}), bf16[96,8192]{1,0:T(8,128)(2,1)}) %all-gather.12.cloned.1.call-update) | async-done | bytes 1572880 | tf_op jit(solution)/shard_map/all_gather | solution.py:70
  20.1 2.4 gather_fusion.4
  22.5 1.0 gather.34
  23.4 24.3 %all-gather.8.cloned.1.call-done = bf16[96,16,32,128]{3,2,1,0:T(8,128)(2,1)} async-done(((bf16[48,16,32,128]{3,2,1,0:T(8,128)(2,1)}), bf16[96,16,32,128]{3,2,1,0:T(8,128)(2,1)}) %all-gather.8.cloned.1.call-update) | async-done | bytes 12582928 | tf_op jit(solution)/shard_map/all_gather | solution.py:69
  47.8 5.3 gather_fusion.2
  53.1 146.8 %all-gather.6.cloned.1.call-done = bf16[640,8192]{1,0:T(8,128)(2,1)} async-done(((bf16[80,8192]{1,0:T(8,128)(2,1)}), bf16[640,8192]{1,0:T(8,128)(2,1)}) %all-gather.6.cloned.1.call-update) | async-done | bytes 10485776 | tf_op jit(solution)/shard_map/all_gather | solution.py:54
  199.9 14.5 %fusion.24 = f32[128,2,640]{0,2,1:T(8,128)S(1)} fusion(bf16[128,2,8192]{2,1,0:T(2,128)(2,1)} %param.13, bf16[640,8192]{1,0:T(8,128)(2,1)} %all-gather.6.cloned.1.call-done), kind=kOutput, calls=%fused_computation.41 | convolution fusion | flops 2684354560 | bytes 15335424 | tf_op jit(solution)/shard_map/ckf,tf->ckt/dot_general | solution.py:103
  214.4 0.8 copy-done.4
  215.3 18.6 %fusion.8 = f32[640,16,128]{2,0,1:T(8,128)} fusion(bf16[16,4096,128]{2,1,0:T(8,128)(2,1)} %param.12, bf16[640,8192]{1,0:T(8,128)(2,1)S(1)} %copy-done.9, s32[]{:T(128)S(6)} %select_n.174), kind=kOutput, calls=%fused_computation.18 | convolution fusion | flops 10737418240 | bytes 27262980 | tf_op jit(solution)/shard_map/tf,mfd->mtd/dot_general | solution.py:95
  233.9 8.1 %all-gather.10.cloned.1.call-done = bf16[96,1024,128]{2,1,0:T(8,128)(2,1)} async-done(((bf16[48,1024,128]{2,1,0:T(8,128)(2,1)}), bf16[96,1024,128]{2,1,0:T(8,128)(2,1)}) %all-gather.10.cloned.1.call-update) | async-done | bytes 25165840 | tf_op jit(solution)/shard_map/all_gather | solution.py:68
  241.9 9.1 %gather_fusion.3 = bf16[8,1024,128]{2,1,0:T(8,128)(2,1)S(1)} fusion(bf16[96,1024,128]{2,1,0:T(8,128)(2,1)} %all-gather.10.cloned.1.call-done, s32[1024]{0:T(1024)S(1)} %pad_clamp_fusion.1), kind=kCustom, calls=%fused_computation.3 | custom fusion | bytes 4194336 | tf_op jit(solution)/shard_map/jit(_take)/gather | solution.py:72
  251.0 1.6 select_bitcast_fusion
  252.6 2.9 copy.30
  255.5 3.7 select_reduce_fusion
  259.2 39.4 %all-reduce.1 = bf16[640,128]{1,0:T(8,128)(2,1)S(1)} all-reduce(f32[640,128]{1,0:T(8,128)} %select_reduce_fusion), channel_id=1, replica_groups=mesh['groups'=2,'replica'=2,'tensor'=8] {'tensor'}, use_global_device_ids=true, to_apply=%region_4.5 | all-reduce | flops 81920 | bytes 491520 | tf_op jit(solution)/shard_map/psum | solution.py:85
  298.5 0.1 slice.35
  298.7 0.1 constant_dynamic-slice_fusion
  298.8 0.1 copy.31
  298.9 5.9 %bitcast_add_fusion = f32[16,640,128]{2,1,0:T(8,128)} fusion(f32[640,16,128]{2,0,1:T(8,128)} %fusion.8, bf16[8,16,32,128]{3,2,1,0:T(8,128)(2,1)S(1)} %gather_fusion.2, pred[8]{0:T(512)(128)(4,1)S(1)} %compare_and_fusion.1, bf16[640,32]{0,1:T(8,128)(2,1)S(1)} %copy.31, bf16[640,8]{0,1:T(8,128)(2,1)S(1)} %get-tuple-element.5), kind=kOutput, calls=%fused_computation.17 | convolution fusion | flops 673087488 | bytes 11585544 | tf_op jit(solution)/shard_map/tj,mjd->mtd/dot_general | solution.py:98
  304.8 2.2 collective-permute-start
  307.1 0.1 copy.34
  307.2 0.6 fusion.31
  307.8 0.8 pad_maximum_fusion
  308.6 0.0 all-gather.14.cloned.1.call-update
  308.7 0.1 convert_reduce_fusion
  308.8 1.7 gather_fusion
  310.5 0.2 fusion.39
  310.8 159.5 %all-gather.14.cloned.1.call-done = bf16[1024,2,640]{0,2,1:T(8,128)(2,1)} async-done(((bf16[128,2,640]{0,2,1:T(8,128)(2,1)}), bf16[1024,2,640]{0,2,1:T(8,128)(2,1)}) %all-gather.14.cloned.1.call-update) | async-done | bytes 2621456 | tf_op jit(solution)/shard_map/all_gather | solution.py:116
  470.3 3.9 copy.45
  474.2 3.8 copy.37
  478.0 3.6 gather_fusion.5
  481.6 5.4 copy_select_fusion
  487.0 69.5 %collective-permute-done = f32[16,640,128]{2,1,0:T(8,128)} collective-permute-done((f32[16,640,128]{2,1,0:T(8,128)}, f32[16,640,128]{2,1,0:T(8,128)}, u32[]{:S(2)}, u32[]{:S(2)}) %collective-permute-start) | collective-permute-done | bytes 5242912 | tf_op jit(solution)/shard_map/ppermute | solution.py:20
  556.5 8.2 %fusion.87 = f32[16,320]{1,0:T(8,128)S(1)} fusion(pred[320,640]{1,0:T(8,128)(4,1)S(1)} %fusion.39, bf16[16,128,2,640]{3,1,0,2:T(8,128)(2,1)} %copy_select_fusion, f32[16,640,128]{2,1,0:T(8,128)} %collective-permute-done, s32[]{:T(128)S(6)} %select_n.188, f32[16,640,128]{2,1,0:T(8,128)} %bitcast_add_fusion), kind=kOutput, calls=%fused_computation.121 | convolution fusion | flops 853279360 | bytes 8089604 | tf_op jit(solution)/shard_map/sub | solution.py:135
  564.7 13.4 %fusion.20 = bf16[1,16,320,128]{3,2,1,0:T(8,128)(2,1)} fusion(bf16[16,128,2,640]{3,1,0,2:T(8,128)(2,1)} %copy_select_fusion, f32[16,320]{1,0:T(8,128)S(1)} %fusion.87, pred[320,640]{1,0:T(8,128)(4,1)S(1)} %fusion.39, f32[16,640,128]{2,1,0:T(8,128)} %collective-permute-done, s32[]{:T(128)S(6)} %select_n.188, f32[16,640,128]{2,1,0:T(8,128)} %bitcast_add_fusion), kind=kOutput, calls=%fused_computation.38 | convolution fusion | flops 1696077440 | bytes 12021764 | tf_op jit(solution)/shard_map/mqk,mdk->mqd/dot_general | solution.py:137
  (35 shorter events, 0.2 us)
Async XLA Ops:
  6.5 4.3 copy-start
  6.5 1.5 copy-start.2
  6.5 1.9 copy-start.6
  6.5 13.6 %all-gather.12.cloned.1.call-start = ((), (), s32[]{:S(2)}) async-start(), calls=%async_computation.3 | async-start | bytes 2359296 | tf_op jit(solution)/shard_map/all_gather | solution.py:70
  7.3 40.5 %all-gather.8.cloned.1.call-start = ((), (), s32[]{:S(2)}) async-start(), calls=%async_computation.1 | async-start | bytes 18874368 | tf_op jit(solution)/shard_map/all_gather | solution.py:69
  8.0 191.9 %all-gather.6.cloned.1.call-start = ((), (), s32[]{:S(2)}) async-start(), calls=%async_computation | async-start | bytes 11796480 | tf_op jit(solution)/shard_map/all_gather | solution.py:54
  9.9 0.7 copy-start.8
  9.9 0.9 copy-start.7
  9.9 232.0 %all-gather.10.cloned.1.call-start = ((), (), s32[]{:S(2)}) async-start(), calls=%async_computation.2 | async-start | bytes 37748736 | tf_op jit(solution)/shard_map/all_gather | solution.py:68
  10.5 459.7 %all-gather.14.cloned.1.call-start = ((), (), s32[]{:S(2)}) async-start(), calls=%async_computation.4 | async-start | bytes 2949120 | tf_op jit(solution)/shard_map/all_gather | solution.py:116
  199.9 15.3 %copy-start.9 = (bf16[640,8192]{1,0:T(8,128)(2,1)S(1)}, bf16[640,8192]{1,0:T(8,128)(2,1)}, u32[]{:S(2)}) copy-start(bf16[640,8192]{1,0:T(8,128)(2,1)} %all-gather.6.cloned.1.call-done) | copy-start | bytes 31457284
  214.4 0.8 copy-start.4
  298.9 8.3 %copy-start.3 = (bf16[8,128,64]{2,1,0:T(8,128)(2,1)S(1)}, bf16[8,128,64]{2,1,0:T(8,128)(2,1)}, u32[]{:S(2)}) copy-start(bf16[8,128,64]{2,1,0:T(8,128)(2,1)} %gather.34) | copy-start | bytes 393220
  298.9 8.3 %copy-start.5 = (f32[128,2,640]{0,2,1:T(8,128)S(1)}, f32[128,2,640]{0,2,1:T(8,128)}, u32[]{:S(2)}) copy-start(f32[128,2,640]{0,2,1:T(8,128)} %copy-done.4) | copy-start | bytes 1966084
  304.8 251.7 %collective-permute-start = (f32[16,640,128]{2,1,0:T(8,128)}, f32[16,640,128]{2,1,0:T(8,128)}, u32[]{:S(2)}, u32[]{:S(2)}) collective-permute-start(f32[16,640,128]{2,1,0:T(8,128)} %bitcast_add_fusion), channel_id=1, source_target_pairs={{0,4},{4,0},{1,5},{5,1},{2,6},{6,2},{3,7},{7,3},{8,12},{12,8},{9,1... | collective-permute-start | bytes 15728648 | tf_op jit(solution)/shard_map/ppermute | solution.py:20
  564.7 13.4 %copy-start.1 = (s32[96]{0:T(128)S(1)}, s32[96]{0:T(128)}, u32[]{:S(2)}) copy-start(s32[96]{0:T(128)} %param.18) | copy-start | bytes 1156
Sparse Core Ops, SparseCore 0:
  8.9 11.1 all-gather.11
  21.7 26.0 all-gather.7
  50.0 149.8 all-gather.5
  201.3 40.5 all-gather.9
  308.7 161.4 all-gather.13
where the time goes:
time: 589 us; the launch traced here: 585 us
  waiting for transfers between devices  419 us (71%)
  matrix products  64.9 us (11%)
  blocking collectives  39.4 us (7%)
  local copies, waits for them, and re-layouts  35.6 us (6%)
  between operations  13.5 us (2%)
  other arithmetic  10.3 us (2%)
    all_gather x1, waiting for transfers between devices, on_device(): key_value_gathered = lax.all_gather(key_value, 'tensor', axis=0, tiled=True)  159 us
    all_gather x1, waiting for transfers between devices, on_device(): gathered_rows = lax.all_gather(normed, 'tensor', axis=0, tiled=True)  147 us
    ppermute x1, waiting for transfers between devices, partner_2(): return lax.ppermute(block, axis, route)  69.5 us
    psum x1, blocking collectives, on_device(): down_bf = lax.psum(partial_down, 'tensor').astype(jnp.bfloat16)  39.4 us
    all_gather x1, waiting for transfers between devices, on_device(): lax.all_gather(adapter_up_query, 'replica', axis=0, tiled=True)  24.3 us
    dot_general x1, matrix products, on_device(): jnp.einsum('tf,mfd->mtd', my_features, query_weight, preferred_element_ty...  18.6 us
    gather x4, local copies, waits for them, and re-layouts, on_device(): jnp.take(store_part, storage_slots, axis=0)  17.7 us
    dot_general x1, matrix products, on_device(): jnp.einsum('ckf,tf->ckt', key_value_weight, gathered_rows, preferred_elem...  14.5 us
  transfers between devices with their start and end apart: 6, of which 6 were waited for; matrix products, arithmetic and copies ran while one was open for 11% of the time, Pallas kernels for 0%

commit v1 on v0

--- a/solution.py
+++ b/solution.py
@@ -140,7 +140,209 @@
     return context[None].astype(jnp.bfloat16)
 
 
+def swap(block, bit):
+    return partner_2(block, "tensor", bit)
+
+
+def side_gather(block, index):
+    count, rest = block.shape[0], block.shape[1:]
+    half = count // 2
+    near = swap(block, 0)
+    far = swap(block, 1)
+    across = jnp.concatenate([swap(near[:half], 1), swap(far[half:], 0)], axis=0)
+    result = jnp.zeros((4 * count,) + rest, block.dtype)
+    for mask, piece in enumerate((block, near, far, across)):
+        result = lax.dynamic_update_slice_in_dim(result, piece, (index ^ mask) * count, 0)
+    return result
+
+
+def fetch_adapters(stores, wanted_pair, adapter_slot, replica_now):
+    held = stores[0].shape[0]
+    count = wanted_pair.shape[1]
+    mine = jnp.take(adapter_slot, lax.dynamic_index_in_dim(wanted_pair, replica_now, 0, keepdims=False))
+    theirs = jnp.take(
+        adapter_slot, lax.dynamic_index_in_dim(wanted_pair, 1 - replica_now, 0, keepdims=False)
+    )
+    base = replica_now * held
+    here = (mine >= base) & (mine < base + held)
+    mine_local = jnp.clip(mine - base, 0, held - 1)
+    theirs_local = jnp.clip(theirs - base, 0, held - 1)
+
+    def pick(store, slots):
+        return jnp.concatenate(
+            [lax.dynamic_slice_in_dim(store, slots[i], 1, 0) for i in range(count)], axis=0
+        )
+
+    result = []
+    for store in stores:
+        received = lax.ppermute(pick(store, theirs_local), "replica", [(0, 1), (1, 0)])
+        keep = here.reshape((count,) + (1,) * (store.ndim - 1))
+        result.append(jnp.where(keep, pick(store, mine_local), received))
+    return result
+
+
+def on_square(
+    tokens,
+    norm_scale_weight,
+    query_weight,
+    key_value_weight,
+    adapter_down_weight,
+    adapter_up_query,
+    adapter_up_value,
+    request_adapter_index,
+    adapter_slot,
+    request_row_lengths,
+):
+    f32, bf = jnp.float32, jnp.bfloat16
+    position = lax.axis_index("tensor")
+    replica_now = lax.axis_index("replica")
+    side, index = position // 4, position % 4
+    rows = tokens.shape[0]
+    side_rows = 4 * rows
+    all_rows = 2 * side_rows
+    window = all_rows // 4
+    half_width = query_weight.shape[1]
+    head_rows = query_weight.shape[0]
+    local_columns = adapter_down_weight.shape[1]
+    rank = adapter_down_weight.shape[2] // 2
+    half_rank = adapter_up_query.shape[2]
+
+    widened = tokens.astype(f32)
+    normed = (
+        widened
+        * lax.rsqrt(jnp.mean(widened * widened, axis=1, keepdims=True) + 1e-05)
+        * norm_scale_weight
+    ).astype(bf)
+    near_half = lax.dynamic_slice_in_dim(normed, side * half_width, half_width, 1)
+    far_half = lax.dynamic_slice_in_dim(normed, (1 - side) * half_width, half_width, 1)
+    other_near = swap(far_half, 2)
+    own_near_all = side_gather(near_half, index)
+    other_near_all = side_gather(other_near, index)
+    other_far = swap(near_half, 2)
+    own_far_all = side_gather(far_half, index)
+    other_far_all = side_gather(other_far, index)
+
+    down_sel, upq_sel, upv_sel = fetch_adapters(
+        (adapter_down_weight, adapter_up_query, adapter_up_value),
+        request_adapter_index,
+        adapter_slot,
+        replica_now,
+    )
+    requests = down_sel.shape[0]
+    upq_other = swap(upq_sel, 2)
+
+    lengths_mine = lax.dynamic_index_in_dim(request_row_lengths, replica_now, 0, keepdims=False)
+    seg_ends = jnp.cumsum(lengths_mine)
+    seg_starts = seg_ends - lengths_mine
+
+    def members(index_of):
+        return (index_of[:, None] >= seg_starts[None, :]) & (index_of[:, None] < seg_ends[None, :])
+
+    line = jnp.arange(side_rows, dtype=jnp.int32)
+    own_index = side * side_rows + line
+    other_index = (1 - side) * side_rows + line
+    own_member, other_member = members(own_index), members(other_index)
+
+    send = jnp.einsum("tf,mfd->mtd", other_near_all, query_weight, preferred_element_type=f32).astype(bf)
+    received = swap(send, 2)
+    own_query = jnp.einsum("tf,mfd->mtd", own_near_all, query_weight, preferred_element_type=f32)
+
+    down_mat = jnp.transpose(down_sel, (1, 0, 2)).reshape(local_columns, requests * 2 * rank)
+
+    def down_part(gathered, member):
+        mine = lax.dynamic_slice_in_dim(gathered, index * local_columns, local_columns, 1)
+        each = jnp.dot(mine, down_mat, preferred_element_type=f32).reshape(
+            side_rows, requests, 2 * rank
+        )
+        return jnp.sum(jnp.where(member[:, :, None], each, f32(0.0)), axis=1)
+
+    down_own = down_part(own_near_all, own_member)
+    down_own = down_own + swap(down_part(other_near_all, other_member), 2)
+    down_own = down_own + swap(down_own, 1)
+    down_own = (down_own + swap(down_own, 0)).astype(bf)
+    down_value_own = down_own[:, rank:]
+    down_value_other = swap(down_value_own, 2)
+
+    def expand(member, values):
+        return (member.astype(bf)[:, :, None] * values[:, None, :]).reshape(
+            values.shape[0], requests * values.shape[1]
+        )
+
+    def up_matrix(selected):
+        return jnp.transpose(selected, (1, 0, 2, 3)).reshape(
+            head_rows, requests * half_rank, HEAD_WIDTH
+        )
+
+    near_ranks = lax.dynamic_slice_in_dim(down_own, side * half_rank, half_rank, 1)
+    far_ranks = lax.dynamic_slice_in_dim(down_own, (1 - side) * half_rank, half_rank, 1)
+    query_up = jnp.einsum(
+        "tj,mjd->mtd",
+        jnp.concatenate([expand(own_member, near_ranks), expand(own_member, far_ranks)], axis=1),
+        jnp.concatenate([up_matrix(upq_sel), up_matrix(upq_other)], axis=1),
+        preferred_element_type=f32,
+    )
+    query = (own_query + query_up + received.astype(f32)).astype(bf)
+
+    kv_near = lax.dynamic_slice_in_dim(key_value_weight, side * half_width, half_width, 2)
+    kv_far = lax.dynamic_slice_in_dim(key_value_weight, (1 - side) * half_width, half_width, 2)
+    upv_mat = jnp.transpose(
+        upv_sel.reshape(requests, HEAD_WIDTH, rank), (0, 2, 1)
+    ).reshape(requests * rank, HEAD_WIDTH)
+
+    def key_values(near, far, member, down_value):
+        base = jnp.einsum("tf,ckf->ktc", near, kv_near, preferred_element_type=f32) + jnp.einsum(
+            "tf,ckf->ktc", far, kv_far, preferred_element_type=f32
+        )
+        up = jnp.dot(expand(member, down_value), upv_mat, preferred_element_type=f32)
+        return jnp.stack([base[0], base[1] + up], axis=0).astype(bf)
+
+    kv_own = key_values(own_near_all, own_far_all, own_member, down_value_own)
+    kv_other = key_values(other_near_all, other_far_all, other_member, down_value_other)
+    kv_rows = jnp.zeros((2, window + all_rows, HEAD_WIDTH), bf)
+    kv_rows = lax.dynamic_update_slice_in_dim(kv_rows, kv_own, window + side * side_rows, 1)
+    kv_rows = lax.dynamic_update_slice_in_dim(kv_rows, kv_other, window + (1 - side) * side_rows, 1)
+    span = window + side_rows
+    for_low, for_high = kv_rows[:, :span], kv_rows[:, side_rows:]
+    odd = position % 2 == 1
+    first = lax.ppermute(
+        jnp.where(odd, for_high, for_low), "tensor", [(c, c // 2 + 4 * (c % 2)) for c in range(8)]
+    )
+    second = lax.ppermute(
+        jnp.where(odd, for_low, for_high), "tensor", [(c, c // 2 + 4 * (1 - c % 2)) for c in range(8)]
+    )
+    even_kv = jnp.where(side == 0, first, second)
+    odd_kv = jnp.where(side == 0, second, first)
+    kv = jnp.stack([even_kv, odd_kv], axis=0)
+
+    blocks = side_rows // window
+    kv = jnp.stack([kv[:, :, b * window : (b + 2) * window] for b in range(blocks)], axis=1)
+    query_index = own_index.reshape(blocks, window)
+    key_index = jnp.stack(
+        [side * side_rows + (b - 1) * window + jnp.arange(2 * window, dtype=jnp.int32) for b in range(blocks)]
+    )
+
+    def segment(index_of):
+        return jnp.sum((index_of[..., None] >= seg_ends).astype(jnp.int32), axis=-1)
+
+    allowed = (
+        (key_index[:, None, :] >= 0)
+        & (key_index[:, None, :] <= query_index[:, :, None])
+        & (segment(key_index)[:, None, :] == segment(query_index)[:, :, None])
+    )
+    query = query.reshape(2, head_rows // 2, blocks, window, HEAD_WIDTH)
+    scores = jnp.einsum(
+        "ghbqd,gbkd->gbhqk", query, kv[:, :, 0], preferred_element_type=f32
+    ) / math.sqrt(HEAD_WIDTH)
+    scores = jnp.where(allowed[None, :, None], scores, f32(-1e30))
+    row_max = jnp.max(scores, axis=-1, keepdims=True)
+    weights = jnp.exp(scores - row_max)
+    weights = (weights / jnp.sum(weights, axis=-1, keepdims=True)).astype(bf)
+    context = jnp.einsum("gbhqk,gbkd->ghbqd", weights, kv[:, :, 1], preferred_element_type=f32)
+    return context.reshape(1, head_rows, side_rows, HEAD_WIDTH).astype(bf)
+
+
 def solution(mesh):
+    square = mesh.shape["tensor"] == KEYVALUE_HEADS
     in_specs = (
         P(("groups", "replica", "tensor"), None),
         P(),
@@ -155,5 +357,5 @@
     )
     out_specs = P(("groups", "replica"), "tensor", None, None)
     return jax.shard_map(
-        on_device, mesh=mesh, in_specs=in_specs, out_specs=out_specs, check_vma=False
-    )
+        on_square if square else on_device, mesh=mesh, in_specs=in_specs, out_specs=out_specs, check_vma=False
+    )

time: 589 us -> 351 us (0.60)
  waiting for transfers between devices: 419 us -> 124 us
  local copies, waits for them, and re-layouts: 35.6 us -> 75.6 us
  starting transfers between devices: 2.38 us -> 42.3 us
  blocking collectives: 39.4 us -> 0 us
  between operations: 13.5 us -> 32.4 us
  matrix products: 64.9 us -> 55.9 us
    all_gather x5 -> x0, waiting for transfers between devices: 347 us -> none  [the longest x1 159 us: on_device(): key_value_gathered = lax.all_gather(key_value, 'tensor', axis=0, tiled=True)]
    ppermute x1 -> x24, waiting for transfers between devices: 69.5 us -> 115 us  [partner_2(): return lax.ppermute(block, axis, route)]
    psum x1 -> x0, blocking collectives: 39.4 us -> none  [on_device(): down_bf = lax.psum(partial_down, 'tensor').astype(jnp.bfloat16)]
    ppermute x1 -> x24, starting transfers between devices: 2.22 us -> 34.7 us  [partner_2(): return lax.ppermute(block, axis, route)]
    unnamed x21 -> x111, local copies, waits for them, and re-layouts: 4.82 us -> 28 us
    gather x7 -> x2, local copies, waits for them, and re-layouts: 23.6 us -> 1.29 us  [the longest x1 0.65 us: fetch_adapters(): jnp.take(adapter_slot, lax.dynamic_index_in_dim(wanted_pair, 1 - replica_...]
    dynamic_slice x2 -> x6, local copies, waits for them, and re-layouts: 0.24 us -> 14.5 us  [the longest x1 8.6 us: on_square(): lax.dynamic_slice_in_dim(key_value_weight, side * half_width, half_width, 2)]
    concatenate x0 -> x5, local copies, waits for them, and re-layouts: none -> 13.8 us  [pick(): jnp.concatenate([lax.dynamic_slice_in_dim(store, slots[i], 1, 0) for i in...]
  transfers between devices with their start and end apart: 6 -> 29, of which waited for: 6 -> 13; matrix products, arithmetic and copies ran while one was open for 11% -> 35% of each run, Pallas kernels for 0% -> 0%
where the time goes in v1:
time: 351 us; the launch traced here: 345 us
  waiting for transfers between devices  124 us (35%)
  local copies, waits for them, and re-layouts  75.6 us (22%)
  matrix products  55.9 us (16%)
  starting transfers between devices  42.3 us (12%)
  between operations  32.4 us (9%)
  other arithmetic  14.6 us (4%)
    ppermute x24, waiting for transfers between devices, partner_2(): return lax.ppermute(block, axis, route)  115 us
    ppermute x24, starting transfers between devices, partner_2(): return lax.ppermute(block, axis, route)  34.7 us
    unnamed x111, local copies, waits for them, and re-layouts  28 us
    concatenate x5, local copies, waits for them, and re-layouts, pick(): jnp.concatenate([lax.dynamic_slice_in_dim(store, slots[i], 1, 0) for i in...  13.8 us
    dot_general x1, matrix products, on_square(): jnp.einsum('tf,mfd->mtd', own_near_all, query_weight, preferred_element_t...  11.1 us
    dot_general x1, matrix products, on_square(): jnp.einsum('tf,mfd->mtd', other_near_all, query_weight, preferred_element...  10.6 us
    dynamic_update_slice x12, local copies, waits for them, and re-layouts, side_gather(): lax.dynamic_update_slice_in_dim(result, piece, (index ^ mask) * count, 0)  8.71 us
    dynamic_slice x1, local copies, waits for them, and re-layouts, on_square(): lax.dynamic_slice_in_dim(key_value_weight, side * half_width, half_width, 2)  8.6 us
  transfers between devices with their start and end apart: 29, of which 13 were waited for; matrix products, arithmetic and copies ran while one was open for 35% of the time, Pallas kernels for 0%

profile of v1, /device:TPU:12, one launch (start us, length us, event | category | flops | bytes accessed | tf_op | source)
XLA Modules:
  0.0 344.9 jit_solution(1594743630137795637)
XLA Ops:
  3.4 1.8 broadcast.243.clone
  8.4 2.6 collective-permute-start.18
  50.8 4.2 %constant_dynamic-slice_fusion.18 = (bf16[1,1024,128]{2,1,0:T(8,128)(2,1)S(1)}, bf16[1,1024,128]{2,1,0:T(8,128)(2,1)S(1)}, bf16[1,1024,128]{2,1,0:T(8,128)(2,1)S...) fusion(bf16[48,1024,128]{2,1,0:T(8,128)(2,1)} %param.16, ...), kind=kLoop, calls=%fused_computation.173 | loop fusion | bytes 8388672 | tf_op jit(solution)/shard_map/dynamic_slice | solution.py:173
  55.0 1.8 copy.128
  58.5 1.8 copy.129
  60.2 1.8 copy.130
  62.0 1.8 copy.131
  63.8 1.8 copy.132
  71.5 8.6 %constant_dynamic-slice_fusion.40 = (bf16[128,2,4096]{2,1,0:T(2,128)(2,1)}, bf16[128,2,4096]{2,1,0:T(2,128)(2,1)}) fusion(bf16[128,2,8192]{2,1,0:T(2,128)(2,1)} %param.15, s32[]{:T(128)S(6)} %select_n.207, s32[]{:T(128)S(6)} %select_n.213), kind=kLoop, calls=%fused_computation.202 | loop fusion | bytes 8388616 | tf_op jit(solution)/shard_map/dynamic_slice | solution.py:286
  80.1 1.8 dynamic-slice_dynamic-update-slice_fusion.7
  82.7 2.1 dynamic-slice_dynamic-update-slice_fusion.6
  84.8 1.7 dynamic-slice_dynamic-update-slice_fusion.5
  86.5 1.8 dynamic-slice_dynamic-update-slice_fusion.4
  93.2 1.7 dynamic-slice_dynamic-update-slice_fusion.1
  94.9 11.1 %concatenate.45 = bf16[8,8192]{1,0:T(8,128)(2,1)S(1)} concatenate(bf16[1,8192]{1,0:T(2,128)(2,1)} %get-tuple-element.58, bf16[1,8192]{1,0:T(2,128)(2,1)} %get-tuple-element.57, bf16[1,8192]{1,0:T(2,128)(2,1)} %get-tuple-element.56, bf16[1,8192]{1,0:T(2,128)(2,1)} %get-tuple-element.55, bf16[1,8192]{1,0:T(2,128)(2,1)S(1)} %copy-done.17, bf16[1,8192]{1,0:T(2,128)(2,1)S(1)} %copy-done.16, ...), dimensions={0} | concatenate | bytes 262144 | tf_op jit(solution)/shard_map/concatenate | solution.py:172
  111.8 2.0 constant_dynamic-update-slice_fusion.26
  113.8 11.7 %collective-permute-done.4 = bf16[80,4096]{1,0:T(8,128)(2,1)} collective-permute-done((bf16[80,4096]{1,0:T(8,128)(2,1)}, bf16[80,4096]{1,0:T(8,128)(2,1)}, u32[]{:S(2)}, u32[]{:S(2)}) %collective-permute-start.4) | collective-permute-done | bytes 655392 | tf_op jit(solution)/shard_map/ppermute | solution.py:20
  129.1 1.7 collective-permute-start.2
  135.9 3.8 %collective-permute-done.2 = bf16[40,4096]{1,0:T(8,128)(2,1)S(1)} collective-permute-done((bf16[40,4096]{1,0:T(8,128)(2,1)S(1)}, bf16[40,4096]{1,0:T(8,128)(2,1)S(1)}, u32[]{:S(2)}, u32[]{:S(2)}) %collective-permute-start.2) | collective-permute-done | bytes 327712 | tf_op jit(solution)/shard_map/ppermute | solution.py:20
  140.3 1.8 collective-permute-done.3
  143.4 11.1 %fusion.21 = f32[320,16,128]{2,0,1:T(8,128)} fusion(bf16[16,4096,128]{2,1,0:T(8,128)(2,1)} %param.14, bf16[320,4096]{1,0:T(8,128)(2,1)} %maximum_dynamic-update-slice_fusion), kind=kOutput, calls=%fused_computation.28 | convolution fusion | flops 5368709120 | bytes 22020096 | tf_op jit(solution)/shard_map/tf,mfd->mtd/dot_general | solution.py:248
  156.3 2.8 fusion.19
  159.1 4.5 %fusion.64 = f32[2,320,128]{2,1,0:T(8,128)S(1)} fusion(f32[128,2,320]{0,2,1:T(8,128)S(1)} %fusion.19, bf16[320,4096]{1,0:T(8,128)(2,1)} %maximum_dynamic-update-slice_fusion, bf16[128,2,4096]{2,1,0:T(2,128)(2,1)S(1)} %copy-done.4), kind=kOutput, calls=%fused_computation.54 | convolution fusion | flops 671170560 | bytes 5373952 | tf_op jit(solution)/shard_map/tf,ckf->ktc/dot_general | solution.py:293
  163.6 2.0 collective-permute-start.20
  167.2 2.6 collective-permute-start.27
  170.0 18.8 %collective-permute-done.11 = bf16[80,4096]{1,0:T(8,128)(2,1)S(1)} collective-permute-done((bf16[80,4096]{1,0:T(8,128)(2,1)}, bf16[80,4096]{1,0:T(8,128)(2,1)S(1)}, u32[]{:S(2)}, u32[]{:S(2)}) %collective-permute-start.11) | collective-permute-done | bytes 655392 | tf_op jit(solution)/shard_map/ppermute | solution.py:20
  188.8 2.4 collective-permute-start.12
  192.6 10.2 %collective-permute-done.20 = bf16[80,4096]{1,0:T(8,128)(2,1)S(1)} collective-permute-done((bf16[80,4096]{1,0:T(8,128)(2,1)}, bf16[80,4096]{1,0:T(8,128)(2,1)S(1)}, u32[]{:S(2)}, u32[]{:S(2)}) %collective-permute-start.20) | collective-permute-done | bytes 655392 | tf_op jit(solution)/shard_map/ppermute | solution.py:20
  202.8 2.4 collective-permute-start.21
  205.3 10.7 %collective-permute-done.12 = bf16[40,4096]{1,0:T(8,128)(2,1)S(1)} collective-permute-done((bf16[40,4096]{1,0:T(8,128)(2,1)S(1)}, bf16[40,4096]{1,0:T(8,128)(2,1)S(1)}, u32[]{:S(2)}, u32[]{:S(2)}) %collective-permute-start.12) | collective-permute-done | bytes 327712 | tf_op jit(solution)/shard_map/ppermute | solution.py:20
  217.6 2.3 collective-permute-done.21
  219.9 3.2 collective-permute-done.22
  223.1 10.6 %fusion.43 = bf16[16,320,128]{2,1,0:T(8,128)(2,1)} fusion(bf16[16,4096,128]{2,1,0:T(8,128)(2,1)} %param.14, bf16[320,4096]{1,0:T(8,128)(2,1)S(1)} %maximum_dynamic-update-slice_fusion.2), kind=kOutput, calls=%fused_computation.47 | convolution fusion | flops 5369364480 | bytes 20709376 | tf_op jit(solution)/shard_map/tf,mfd->mtd/dot_general | solution.py:246
  235.0 2.6 collective-permute-start.14
  237.6 2.6 fusion.56
  240.2 2.4 collective-permute-done.14
  243.4 2.7 fusion.13
  246.1 1.9 collective-permute-done.15
  249.7 2.7 fusion.74
  252.4 3.6 %collective-permute-start.28 = (bf16[16,320,128]{2,1,0:T(8,128)(2,1)}, bf16[16,320,128]{2,1,0:T(8,128)(2,1)}, u32[]{:S(2)}, u32[]{:S(2)}) collective-permute-start(bf16[16,320,128]{2,1,0:T(8,128)(2,1)} %fusion.43), channel_id=1, source_target_pairs={{0,4},{4,0},{1,5},{5,1},{2,6},{6,2},{3,7},{7,3},{8,12},{12,8},{9,1... | collective-permute-start | bytes 3932168 | tf_op jit(solution)/shard_map/ppermute | solution.py:20
  258.3 48.7 %collective-permute-done.23 = bf16[320,64]{1,0:T(8,128)(2,1)S(1)} collective-permute-done((bf16[320,64]{1,0:T(8,128)(2,1)S(1)}, bf16[320,64]{1,0:T(8,128)(2,1)S(1)}, u32[]{:S(2)}, u32[]{:S(2)}) %collective-permute-start.23) | collective-permute-done | bytes 40992 | tf_op jit(solution)/shard_map/ppermute | solution.py:20
  309.2 4.5 %collective-permute-start.24 = (bf16[2,480,128]{2,1,0:T(8,128)(2,1)}, bf16[2,480,128]{2,1,0:T(8,128)(2,1)S(1)}, u32[]{:S(2)}, u32[]{:S(2)}) collective-permute-start(bf16[2,480,128]{2,1,0:T(8,128)(2,1)} %get-tuple-element.64), channel_id=1, source_target_pairs={{0,0},{1,4},{2,1},{3,5},{4,2},{5,6},{6,3},{7,7},{8,8},{9,12},{10,9... | collective-permute-start | bytes 737288 | tf_op jit(solution)/shard_map/ppermute | solution.py:307
  313.7 2.5 collective-permute-start.25
  316.9 6.5 %collective-permute-done.24 = bf16[2,480,128]{2,1,0:T(8,128)(2,1)S(1)} collective-permute-done((bf16[2,480,128]{2,1,0:T(8,128)(2,1)}, bf16[2,480,128]{2,1,0:T(8,128)(2,1)S(1)}, u32[]{:S(2)}, u32[]{:S(2)}) %collective-permute-start.24) | collective-permute-done | bytes 245792 | tf_op jit(solution)/shard_map/ppermute | solution.py:307
  323.4 2.1 collective-permute-done.25
  327.2 4.1 %fusion.12 = bf16[16,320,128]{2,1,0:T(8,128)(2,1)} fusion(f32[320,16,128]{2,0,1:T(8,128)} %fusion.21, bf16[16,320,128]{2,1,0:T(8,128)(2,1)} %collective-permute-done.28, bf16[16,256,128]{2,1,0:T(8,128)(2,1)S(1)} %bitcast.185, bf16[16,256,128]{2,1,0:T(8,128)(2,1)S(1)} %bitcast.184, bf16[320,256]{1,0:T(8,128)(2,1)S(1)} %copy.111, bf16[320,256]{1,0:T(8,128)(2,1)S(1)} %copy.110), kind=kOutput, calls=%fused_computation.19 | convolution fusion | flops 678559744 | bytes 7667712 | tf_op jit(solution)/shard_map/tj,mjd->mtd/dot_general | solution.py:278
  331.4 7.4 %fusion.135 = (f32[2,2,8,160]{3,2,1,0:T(8,128)S(1)}, f32[2,2,8,160,320]{4,3,2,1,0:T(8,128)}) fusion(pred[2,160,320]{2,1,0:T(8,128)(4,1)S(1)} %copy-done.18, bf16[2,8,2,160,128]{4,3,2,1,0:T(8,128)(2,1)} %bitcast.186, bf16[2,1,2,320,128]{4,3,1,0,2:T(8,128)(2,1)S(1)} %copy-done.12, bf16[2,1,2,320,128]{4,3,1,0,2:T(8,128)(2,1)S(1)} %get-tuple-element.60), kind=kOutput, calls=%fused_computation.238 | convolution fusion | flops 426148160 | bytes 8642560 | tf_op jit(solution)/shard_map/sub | solution.py:338
  338.8 4.5 %fusion.46 = bf16[2,8,2,160,128]{4,3,1,2,0:T(8,128)(2,1)S(1)} fusion(f32[2,2,8,160,320]{4,3,2,1,0:T(8,128)} %get-tuple-element.95, f32[2,2,8,160]{3,2,1,0:T(8,128)S(1)} %get-tuple-element.94, bf16[2,1,2,320,128]{4,3,1,0,2:T(8,128)(2,1)S(1)} %get-tuple-element.60, bf16[2,1,2,320,128]{4,3,1,0,2:T(8,128)(2,1)S(1)} %copy-done.12), kind=kOutput, calls=%fused_computation.48 | convolution fusion | flops 424017920 | bytes 8540160 | tf_op jit(solution)/shard_map/gbhqk,gbkd->ghbqd/dot_general | solution.py:340
  (220 shorter events, 62.8 us)
Async XLA Ops:
  0.0 14.0 %copy-start = (s32[96]{0:T(128)S(1)}, s32[96]{0:T(128)}, u32[]{:S(2)}) copy-start(s32[96]{0:T(128)} %param.20) | copy-start | bytes 1156
  6.4 103.8 %collective-permute-start = (bf16[80,4096]{1,0:T(8,128)(2,1)}, bf16[80,4096]{1,0:T(8,128)(2,1)}, u32[]{:S(2)}, u32[]{:S(2)}) collective-permute-start(bf16[80,4096]{1,0:T(8,128)(2,1)} %get-tuple-element.9), channel_id=1, source_target_pairs={{0,1},{1,0},{2,3},{3,2},{4,5},{5,4},{6,7},{7,6},{8,9},{9,8},{10,11... | collective-permute-start | bytes 1966088 | tf_op jit(solution)/shard_map/ppermute | solution.py:20
  7.9 118.7 %collective-permute-start.1 = (bf16[80,4096]{1,0:T(8,128)(2,1)}, bf16[80,4096]{1,0:T(8,128)(2,1)S(1)}, u32[]{:S(2)}, u32[]{:S(2)}) collective-permute-start(bf16[80,4096]{1,0:T(8,128)(2,1)} %get-tuple-element.9), channel_id=1, source_target_pairs={{0,2},{2,0},{1,3},{3,1},{4,6},{6,4},{5,7},{7,5},{8,10},{10,8},{9,1... | collective-permute-start | bytes 1966088 | tf_op jit(solution)/shard_map/ppermute | solution.py:20
  8.4 125.6 %collective-permute-start.18 = (bf16[80,4096]{1,0:T(8,128)(2,1)}, bf16[80,4096]{1,0:T(8,128)(2,1)}, u32[]{:S(2)}, u32[]{:S(2)}) collective-permute-start(bf16[80,4096]{1,0:T(8,128)(2,1)} %get-tuple-element.9), channel_id=1, source_target_pairs={{0,4},{4,0},{1,5},{5,1},{2,6},{6,2},{3,7},{7,3},{8,12},{12,8},{9,1... | collective-permute-start | bytes 1966088 | tf_op jit(solution)/shard_map/ppermute | solution.py:20
  10.9 36.7 %copy-start.11 = (bf16[48,8192]{1,0:T(8,128)(2,1)S(1)}, bf16[48,8192]{1,0:T(8,128)(2,1)}, u32[]{:S(2)}) copy-start(bf16[48,8192]{1,0:T(8,128)(2,1)} %param.18) | copy-start | bytes 2359300
  13.7 118.3 %collective-permute-start.9 = (bf16[80,4096]{1,0:T(8,128)(2,1)}, bf16[80,4096]{1,0:T(8,128)(2,1)}, u32[]{:S(2)}, u32[]{:S(2)}) collective-permute-start(bf16[80,4096]{1,0:T(8,128)(2,1)} %get-tuple-element.7), channel_id=1, source_target_pairs={{0,4},{4,0},{1,5},{5,1},{2,6},{6,2},{3,7},{7,3},{8,12},{12,8},{9,1... | collective-permute-start | bytes 1966088 | tf_op jit(solution)/shard_map/ppermute | solution.py:20
  14.7 36.1 %copy-start.31 = (s32[8]{0:T(128)}, s32[8]{0:T(128)S(1)}, u32[]{:S(2)}) copy-start(s32[8]{0:T(128)S(1)} %gather_fusion) | copy-start | bytes 100
  50.2 57.5 %collective-permute-start.17 = (bf16[8,8192]{1,0:T(8,128)(2,1)}, bf16[8,8192]{1,0:T(8,128)(2,1)}, u32[]{:S(2)}, u32[]{:S(2)}) collective-permute-start(bf16[8,8192]{1,0:T(8,128)(2,1)} %concatenate.46), channel_id=1, source_target_pairs={{0,8},{8,0},{1,9},{9,1},{2,10},{10,2},{3,11},{11,3},{4,12},{12,4},... | collective-permute-start | bytes 393224 | tf_op jit(solution)/shard_map/ppermute | solution.py:178
  69.6 12.5 %copy-start.27 = (s32[8,1]{0,1:T(1,128)}, s32[8,1]{0,1:T(1,128)S(1)}, u32[]{:S(2)}) copy-start(s32[8,1]{0,1:T(1,128)S(1)} %reduce-window.4) | copy-start | bytes 100
  71.5 10.7 %copy-start.9 = (bf16[1,1024,128]{1,2,0:T(8,128)(2,1)S(1)}, bf16[1,1024,128]{1,2,0:T(8,128)(2,1)}, u32[]{:S(2)}) copy-start(bf16[1,1024,128]{1,2,0:T(8,128)(2,1)} %copy.129) | copy-start | bytes 786436
  71.5 10.7 %copy-start.22 = (bf16[8,1024,128]{1,2,0:T(8,128)(2,1)S(1)}, bf16[8,1024,128]{1,2,0:T(8,128)(2,1)}, u32[]{:S(2)}) copy-start(bf16[8,1024,128]{1,2,0:T(8,128)(2,1)} %constant_dynamic-update-slice_fusion.15) | copy-start | bytes 6291460
  71.5 10.7 %copy-start.10 = (bf16[1,1024,128]{1,2,0:T(8,128)(2,1)S(1)}, bf16[1,1024,128]{1,2,0:T(8,128)(2,1)}, u32[]{:S(2)}) copy-start(bf16[1,1024,128]{1,2,0:T(8,128)(2,1)} %copy.130) | copy-start | bytes 786436
  71.5 10.7 %copy-start.8 = (bf16[1,1024,128]{1,2,0:T(8,128)(2,1)S(1)}, bf16[1,1024,128]{1,2,0:T(8,128)(2,1)}, u32[]{:S(2)}) copy-start(bf16[1,1024,128]{1,2,0:T(8,128)(2,1)} %copy.131) | copy-start | bytes 786436
  71.5 10.8 %copy-start.7 = (bf16[1,1024,128]{1,2,0:T(8,128)(2,1)S(1)}, bf16[1,1024,128]{1,2,0:T(8,128)(2,1)}, u32[]{:S(2)}) copy-start(bf16[1,1024,128]{1,2,0:T(8,128)(2,1)} %copy.132) | copy-start | bytes 786436
  82.5 9.9 %copy-start.29 = (pred[2,320]{1,0:T(4,128)(4,1)S(1)}, pred[2,320]{1,0:T(4,128)(4,1)}, u32[]{:S(2)}) copy-start(pred[2,320]{1,0:T(4,128)(4,1)} %broadcast_compare_fusion) | copy-start | bytes 1924
  82.6 12.3 %copy-start.14 = (bf16[1,8192]{1,0:T(2,128)(2,1)S(1)}, bf16[1,8192]{1,0:T(2,128)(2,1)}, u32[]{:S(2)}) copy-start(bf16[1,8192]{1,0:T(2,128)(2,1)} %get-tuple-element.51) | copy-start | bytes 49156
  82.6 12.3 %copy-start.15 = (bf16[1,8192]{1,0:T(2,128)(2,1)S(1)}, bf16[1,8192]{1,0:T(2,128)(2,1)}, u32[]{:S(2)}) copy-start(bf16[1,8192]{1,0:T(2,128)(2,1)} %get-tuple-element.52) | copy-start | bytes 49156
  82.6 12.3 %copy-start.16 = (bf16[1,8192]{1,0:T(2,128)(2,1)S(1)}, bf16[1,8192]{1,0:T(2,128)(2,1)}, u32[]{:S(2)}) copy-start(bf16[1,8192]{1,0:T(2,128)(2,1)} %get-tuple-element.53) | copy-start | bytes 49156
  82.6 12.3 %copy-start.17 = (bf16[1,8192]{1,0:T(2,128)(2,1)S(1)}, bf16[1,8192]{1,0:T(2,128)(2,1)}, u32[]{:S(2)}) copy-start(bf16[1,8192]{1,0:T(2,128)(2,1)} %get-tuple-element.54) | copy-start | bytes 49156
  86.5 39.0 %copy-start.3 = (bf16[320,4096]{1,0:T(8,128)(2,1)S(1)}, bf16[320,4096]{1,0:T(8,128)(2,1)}, u32[]{:S(2)}) copy-start(bf16[320,4096]{1,0:T(8,128)(2,1)} %copy-done.2) | copy-start | bytes 7864324
  107.7 17.8 %collective-permute-start.4 = (bf16[80,4096]{1,0:T(8,128)(2,1)}, bf16[80,4096]{1,0:T(8,128)(2,1)}, u32[]{:S(2)}, u32[]{:S(2)}) collective-permute-start(bf16[80,4096]{1,0:T(8,128)(2,1)} %get-tuple-element.7), channel_id=1, source_target_pairs={{0,1},{1,0},{2,3},{3,2},{4,5},{5,4},{6,7},{7,6},{8,9},{9,8},{10,11... | collective-permute-start | bytes 1966088 | tf_op jit(solution)/shard_map/ppermute | solution.py:20
  110.2 18.9 %collective-permute-start.5 = (bf16[80,4096]{1,0:T(8,128)(2,1)}, bf16[80,4096]{1,0:T(8,128)(2,1)S(1)}, u32[]{:S(2)}, u32[]{:S(2)}) collective-permute-start(bf16[80,4096]{1,0:T(8,128)(2,1)} %get-tuple-element.7), channel_id=1, source_target_pairs={{0,2},{2,0},{1,3},{3,1},{4,6},{6,4},{5,7},{7,5},{8,10},{10,8},{9,1... | collective-permute-start | bytes 1966088 | tf_op jit(solution)/shard_map/ppermute | solution.py:20
  125.5 108.2 %collective-permute-start.8 = (bf16[8,1024,128]{1,2,0:T(8,128)(2,1)}, bf16[8,1024,128]{1,2,0:T(8,128)(2,1)S(1)}, u32[]{:S(2)}, u32[]{:S(2)}) collective-permute-start(bf16[8,1024,128]{1,2,0:T(8,128)(2,1)} %copy-done.23), channel_id=1, source_target_pairs={{0,8},{8,0},{1,9},{9,1},{2,10},{10,2},{3,11},{11,3},{4,12},{12,4},... | collective-permute-start | bytes 6291464 | tf_op jit(solution)/shard_map/ppermute | solution.py:178
  126.6 37.0 %collective-permute-start.26 = (bf16[8,16,32,128]{3,2,1,0:T(8,128)(2,1)}, bf16[8,16,32,128]{3,2,1,0:T(8,128)(2,1)S(1)}, u32[]{:S(2)}, u32[]{:S(2)}) collective-permute-start(bf16[8,16,32,128]{3,2,1,0:T(8,128)(2,1)} %get-tuple-element.26), channel_id=1, source_target_pairs={{0,8},{8,0},{1,9},{9,1},{2,10},{10,2},{3,11},{11,3},{4,12},{12,4},... | collective-permute-start | bytes 3145736 | tf_op jit(solution)/shard_map/ppermute | solution.py:178
  129.1 10.6 %collective-permute-start.2 = (bf16[40,4096]{1,0:T(8,128)(2,1)S(1)}, bf16[40,4096]{1,0:T(8,128)(2,1)S(1)}, u32[]{:S(2)}, u32[]{:S(2)}) collective-permute-start(bf16[40,4096]{1,0:T(8,128)(2,1)S(1)} %slice.178), channel_id=1, source_target_pairs={{0,2},{2,0},{1,3},{3,1},{4,6},{6,4},{5,7},{7,5},{8,10},{10,8},{9,1... | collective-permute-start | bytes 983048 | tf_op jit(solution)/shard_map/ppermute | solution.py:20
  131.9 10.1 %collective-permute-start.3 = (bf16[40,4096]{1,0:T(8,128)(2,1)S(1)}, bf16[40,4096]{1,0:T(8,128)(2,1)S(1)}, u32[]{:S(2)}, u32[]{:S(2)}) collective-permute-start(bf16[40,4096]{1,0:T(8,128)(2,1)S(1)} %slice.179), channel_id=1, source_target_pairs={{0,1},{1,0},{2,3},{3,2},{4,5},{5,4},{6,7},{7,6},{8,9},{9,8},{10,11... | collective-permute-start | bytes 983048 | tf_op jit(solution)/shard_map/ppermute | solution.py:20
  134.0 20.6 %collective-permute-start.6 = (bf16[40,4096]{1,0:T(8,128)(2,1)S(1)}, bf16[40,4096]{1,0:T(8,128)(2,1)S(1)}, u32[]{:S(2)}, u32[]{:S(2)}) collective-permute-start(bf16[40,4096]{1,0:T(8,128)(2,1)S(1)} %slice.180), channel_id=1, source_target_pairs={{0,2},{2,0},{1,3},{3,1},{4,6},{6,4},{5,7},{7,5},{8,10},{10,8},{9,1... | collective-permute-start | bytes 983048 | tf_op jit(solution)/shard_map/ppermute | solution.py:20
  139.7 15.7 %collective-permute-start.7 = (bf16[40,4096]{1,0:T(8,128)(2,1)S(1)}, bf16[40,4096]{1,0:T(8,128)(2,1)S(1)}, u32[]{:S(2)}, u32[]{:S(2)}) collective-permute-start(bf16[40,4096]{1,0:T(8,128)(2,1)S(1)} %slice.181), channel_id=1, source_target_pairs={{0,1},{1,0},{2,3},{3,2},{4,5},{5,4},{6,7},{7,6},{8,9},{9,8},{10,11... | collective-permute-start | bytes 983048 | tf_op jit(solution)/shard_map/ppermute | solution.py:20
  142.1 25.1 %collective-permute-start.10 = (bf16[80,4096]{1,0:T(8,128)(2,1)}, bf16[80,4096]{1,0:T(8,128)(2,1)S(1)}, u32[]{:S(2)}, u32[]{:S(2)}) collective-permute-start(bf16[80,4096]{1,0:T(8,128)(2,1)} %collective-permute-done.9), channel_id=1, source_target_pairs={{0,1},{1,0},{2,3},{3,2},{4,5},{5,4},{6,7},{7,6},{8,9},{9,8},{10,11... | collective-permute-start | bytes 1966088 | tf_op jit(solution)/shard_map/ppermute | solution.py:20
  143.4 12.8 %copy-start.5 = (bf16[128,2,4096]{2,1,0:T(2,128)(2,1)S(1)}, bf16[128,2,4096]{2,1,0:T(2,128)(2,1)}, u32[]{:S(2)}) copy-start(bf16[128,2,4096]{2,1,0:T(2,128)(2,1)} %get-tuple-element.43) | copy-start | bytes 6291460
  154.5 34.2 %collective-permute-start.11 = (bf16[80,4096]{1,0:T(8,128)(2,1)}, bf16[80,4096]{1,0:T(8,128)(2,1)S(1)}, u32[]{:S(2)}, u32[]{:S(2)}) collective-permute-start(bf16[80,4096]{1,0:T(8,128)(2,1)} %collective-permute-done.9), channel_id=1, source_target_pairs={{0,2},{2,0},{1,3},{3,1},{4,6},{6,4},{5,7},{7,5},{8,10},{10,8},{9,1... | collective-permute-start | bytes 1966088 | tf_op jit(solution)/shard_map/ppermute | solution.py:20
  155.4 35.8 %collective-permute-start.19 = (bf16[80,4096]{1,0:T(8,128)(2,1)}, bf16[80,4096]{1,0:T(8,128)(2,1)S(1)}, u32[]{:S(2)}, u32[]{:S(2)}) collective-permute-start(bf16[80,4096]{1,0:T(8,128)(2,1)} %collective-permute-done.18), channel_id=1, source_target_pairs={{0,1},{1,0},{2,3},{3,2},{4,5},{5,4},{6,7},{7,6},{8,9},{9,8},{10,11... | collective-permute-start | bytes 1966088 | tf_op jit(solution)/shard_map/ppermute | solution.py:20
  163.6 39.2 %collective-permute-start.20 = (bf16[80,4096]{1,0:T(8,128)(2,1)}, bf16[80,4096]{1,0:T(8,128)(2,1)S(1)}, u32[]{:S(2)}, u32[]{:S(2)}) collective-permute-start(bf16[80,4096]{1,0:T(8,128)(2,1)} %collective-permute-done.18), channel_id=1, source_target_pairs={{0,2},{2,0},{1,3},{3,1},{4,6},{6,4},{5,7},{7,5},{8,10},{10,8},{9,1... | collective-permute-start | bytes 1966088 | tf_op jit(solution)/shard_map/ppermute | solution.py:20
  167.2 88.8 %collective-permute-start.27 = (bf16[8,16,32,128]{3,2,1,0:T(8,128)(2,1)S(1)}, bf16[8,16,32,128]{3,2,1,0:T(8,128)(2,1)S(1)}, u32[]{:S(2)}, u32[]{:S(2)}) collective-permute-start(bf16[8,16,32,128]{3,2,1,0:T(8,128)(2,1)S(1)} %broadcast_select_fusion.1), channel_id=1, source_target_pairs={{0,4},{4,0},{1,5},{5,1},{2,6},{6,2},{3,7},{7,3},{8,12},{12,8},{9,1... | collective-permute-start | bytes 3145736 | tf_op jit(solution)/shard_map/ppermute | solution.py:20
  188.8 27.2 %collective-permute-start.12 = (bf16[40,4096]{1,0:T(8,128)(2,1)S(1)}, bf16[40,4096]{1,0:T(8,128)(2,1)S(1)}, u32[]{:S(2)}, u32[]{:S(2)}) collective-permute-start(bf16[40,4096]{1,0:T(8,128)(2,1)S(1)} %slice.184), channel_id=1, source_target_pairs={{0,2},{2,0},{1,3},{3,1},{4,6},{6,4},{5,7},{7,5},{8,10},{10,8},{9,1... | collective-permute-start | bytes 983048 | tf_op jit(solution)/shard_map/ppermute | solution.py:20
  191.2 26.3 %collective-permute-start.13 = (bf16[40,4096]{1,0:T(8,128)(2,1)S(1)}, bf16[40,4096]{1,0:T(8,128)(2,1)S(1)}, u32[]{:S(2)}, u32[]{:S(2)}) collective-permute-start(bf16[40,4096]{1,0:T(8,128)(2,1)S(1)} %slice.185), channel_id=1, source_target_pairs={{0,1},{1,0},{2,3},{3,2},{4,5},{5,4},{6,7},{7,6},{8,9},{9,8},{10,11... | collective-permute-start | bytes 983048 | tf_op jit(solution)/shard_map/ppermute | solution.py:20
  202.8 17.1 %collective-permute-start.21 = (bf16[40,4096]{1,0:T(8,128)(2,1)S(1)}, bf16[40,4096]{1,0:T(8,128)(2,1)S(1)}, u32[]{:S(2)}, u32[]{:S(2)}) collective-permute-start(bf16[40,4096]{1,0:T(8,128)(2,1)S(1)} %slice.187), channel_id=1, source_target_pairs={{0,2},{2,0},{1,3},{3,1},{4,6},{6,4},{5,7},{7,5},{8,10},{10,8},{9,1... | collective-permute-start | bytes 983048 | tf_op jit(solution)/shard_map/ppermute | solution.py:20
  216.0 7.1 %collective-permute-start.22 = (bf16[40,4096]{1,0:T(8,128)(2,1)S(1)}, bf16[40,4096]{1,0:T(8,128)(2,1)S(1)}, u32[]{:S(2)}, u32[]{:S(2)}) collective-permute-start(bf16[40,4096]{1,0:T(8,128)(2,1)S(1)} %slice.188), channel_id=1, source_target_pairs={{0,1},{1,0},{2,3},{3,2},{4,5},{5,4},{6,7},{7,6},{8,9},{9,8},{10,11... | collective-permute-start | bytes 983048 | tf_op jit(solution)/shard_map/ppermute | solution.py:20
  223.1 10.6 %copy-start.21 = (bf16[8,1024,128]{1,2,0:T(8,128)(2,1)S(1)}, bf16[8,1024,128]{1,2,0:T(8,128)(2,1)}, u32[]{:S(2)}) copy-start(bf16[8,1024,128]{1,2,0:T(8,128)(2,1)} %copy-done.20) | copy-start | bytes 6291460
  223.1 10.6 %copy-start.34 = (pred[320,8]{0,1:T(8,128)(4,1)S(1)}, pred[320,8]{0,1:T(8,128)(4,1)}, u32[]{:S(2)}) copy-start(pred[320,8]{0,1:T(8,128)(4,1)} %get-tuple-element.71) | copy-start | bytes 7684
  235.0 7.6 %collective-permute-start.14 = (f32[320,128]{1,0:T(8,128)S(1)}, f32[320,128]{1,0:T(8,128)S(1)}, u32[]{:S(2)}, u32[]{:S(2)}) collective-permute-start(f32[320,128]{1,0:T(8,128)S(1)} %fusion.53), channel_id=1, source_target_pairs={{0,4},{4,0},{1,5},{5,1},{2,6},{6,2},{3,7},{7,3},{8,12},{12,8},{9,1... | collective-permute-start | bytes 491528 | tf_op jit(solution)/shard_map/ppermute | solution.py:20
  242.6 5.4 %collective-permute-start.15 = (f32[320,128]{1,0:T(8,128)S(1)}, f32[320,128]{1,0:T(8,128)S(1)}, u32[]{:S(2)}, u32[]{:S(2)}) collective-permute-start(f32[320,128]{1,0:T(8,128)S(1)} %add.306), channel_id=1, source_target_pairs={{0,2},{2,0},{1,3},{3,1},{4,6},{6,4},{5,7},{7,5},{8,10},{10,8},{9,1... | collective-permute-start | bytes 491528 | tf_op jit(solution)/shard_map/ppermute | solution.py:20
  248.0 8.1 %collective-permute-start.16 = (f32[320,128]{1,0:T(8,128)S(1)}, f32[320,128]{1,0:T(8,128)S(1)}, u32[]{:S(2)}, u32[]{:S(2)}) collective-permute-start(f32[320,128]{1,0:T(8,128)S(1)} %add.307), channel_id=1, source_target_pairs={{0,1},{1,0},{2,3},{3,2},{4,5},{5,4},{6,7},{7,6},{8,9},{9,8},{10,11... | collective-permute-start | bytes 491528 | tf_op jit(solution)/shard_map/ppermute | solution.py:20
  252.4 54.7 %copy-start.30 = (bf16[320,8]{0,1:T(8,128)(2,1)S(1)}, bf16[320,8]{0,1:T(8,128)(2,1)}, u32[]{:S(2)}) copy-start(bf16[320,8]{0,1:T(8,128)(2,1)} %get-tuple-element.70) | copy-start | bytes 15364
  252.4 74.8 %collective-permute-start.28 = (bf16[16,320,128]{2,1,0:T(8,128)(2,1)}, bf16[16,320,128]{2,1,0:T(8,128)(2,1)}, u32[]{:S(2)}, u32[]{:S(2)}) collective-permute-start(bf16[16,320,128]{2,1,0:T(8,128)(2,1)} %fusion.43), channel_id=1, source_target_pairs={{0,4},{4,0},{1,5},{5,1},{2,6},{6,2},{3,7},{7,3},{8,12},{12,8},{9,1... | collective-permute-start | bytes 3932168 | tf_op jit(solution)/shard_map/ppermute | solution.py:20
  256.2 50.7 %collective-permute-start.23 = (bf16[320,64]{1,0:T(8,128)(2,1)S(1)}, bf16[320,64]{1,0:T(8,128)(2,1)S(1)}, u32[]{:S(2)}, u32[]{:S(2)}) collective-permute-start(bf16[320,64]{1,0:T(8,128)(2,1)S(1)} %slice.186), channel_id=1, source_target_pairs={{0,4},{4,0},{1,5},{5,1},{2,6},{6,2},{3,7},{7,3},{8,12},{12,8},{9,1... | collective-permute-start | bytes 122888 | tf_op jit(solution)/shard_map/ppermute | solution.py:20
  309.2 14.2 %collective-permute-start.24 = (bf16[2,480,128]{2,1,0:T(8,128)(2,1)}, bf16[2,480,128]{2,1,0:T(8,128)(2,1)S(1)}, u32[]{:S(2)}, u32[]{:S(2)}) collective-permute-start(bf16[2,480,128]{2,1,0:T(8,128)(2,1)} %get-tuple-element.64), channel_id=1, source_target_pairs={{0,0},{1,4},{2,1},{3,5},{4,2},{5,6},{6,3},{7,7},{8,8},{9,12},{10,9... | collective-permute-start | bytes 737288 | tf_op jit(solution)/shard_map/ppermute | solution.py:307
  313.7 11.8 %collective-permute-start.25 = (bf16[2,480,128]{2,1,0:T(8,128)(2,1)S(1)}, bf16[2,480,128]{2,1,0:T(8,128)(2,1)}, u32[]{:S(2)}, u32[]{:S(2)}) collective-permute-start(bf16[2,480,128]{2,1,0:T(8,128)(2,1)S(1)} %get-tuple-element.65), channel_id=1, source_target_pairs={{0,4},{1,0},{2,5},{3,1},{4,6},{5,2},{6,7},{7,3},{8,12},{9,8},{10,1... | collective-permute-start | bytes 737288 | tf_op jit(solution)/shard_map/ppermute | solution.py:310
  (18 other events, 89.8 us)
